TPU v7x, 1024 devices: a whole 8x8x8 slice. The times are simulated.
1024 devices in a mesh: prow: 64 (over x, z), pcol: 16 (over y, core).
Axes of the slice: x: 8, y: 8, z: 8, core: 2. Of those that a mesh axis runs over, the one named last changes fastest.
Arguments:
- rhs_first: float32 [8192, 256], P('prow'), may hold values from -6 to 6
- rhs_second: float32 [8192, 256], P('prow'), may hold values from -6 to 6
- rhs_rest: float32 [90112, 256], P(('prow', 'pcol')), may hold values from -6 to 6
- inverse_first: bfloat16 [8192, 8192], P('pcol', 'prow'), as said below
- inverse_second: bfloat16 [8192, 8192], P('pcol', 'prow'), as said below
- panel_cross: bfloat16 [8192, 8192], P('prow', 'pcol'), may hold values from -0.0625 to 0.0625
- panel_first_rest: bfloat16 [90112, 8192], P('prow', 'pcol'), may hold values from -0.1875 to 0.1875
- panel_second_rest: bfloat16 [90112, 8192], P('prow', 'pcol'), may hold values from -0.1875 to 0.1875
Outputs:
- solved_first: float32 [8192, 256], P('pcol')
- solved_second: float32 [8192, 256], P('pcol')
- remaining: float32 [90112, 256], P(('prow', 'pcol'))
Inputs may be any that keep to these rules, and one draw needn't show every extreme that they name: `inverse_first`: lower triangular: entry (i, j) is zero for j > i; the diagonal entries lie between 1 and 2. `inverse_second`: lower triangular: entry (i, j) is zero for j > i; the diagonal entries lie between 1 and 2.
All inputs are finite; a program needn't handle non-finite values.
Results may differ from a plain program's by a relative error of at most 0.005.
Values sent between devices are 32-bit elements; how exact they have to be, the bound alone decides.
A program may use at most 32 MiB of HBM per device.

v0:
```python
import jax
import jax.numpy as jnp
from jax import lax
from jax.sharding import PartitionSpec as P


def solve_block(inverse_local, block_values):
    partial_value = jnp.dot(
        inverse_local, block_values.astype(jnp.bfloat16), preferred_element_type=jnp.float32
    )
    return lax.psum(partial_value, "prow")


def local(
    rhs_first,
    rhs_second,
    rhs_rest,
    inverse_first,
    inverse_second,
    panel_cross,
    panel_first_rest,
    panel_second_rest,
):
    solved_first = solve_block(inverse_first, rhs_first)
    first_rounded = solved_first.astype(jnp.bfloat16)
    crossing = jnp.dot(panel_cross, first_rounded, preferred_element_type=jnp.float32)
    second_rows = rhs_second - lax.psum(crossing, "pcol")
    solved_second = solve_block(inverse_second, second_rows)
    second_rounded = solved_second.astype(jnp.bfloat16)

    def trailing_update(factor_rows, solved):
        return lax.psum_scatter(
            jnp.dot(factor_rows, solved, preferred_element_type=jnp.float32),
            "pcol",
            scatter_dimension=0,
            tiled=True,
        )

    remaining = rhs_rest - trailing_update(panel_first_rest, first_rounded)
    remaining = remaining - trailing_update(panel_second_rest, second_rounded)
    return (solved_first, solved_second, remaining)


def solution(mesh):
    in_specs = (
        P("prow", None),
        P("prow", None),
        P(("prow", "pcol"), None),
        P("pcol", "prow"),
        P("pcol", "prow"),
        P("prow", "pcol"),
        P("prow", "pcol"),
        P("prow", "pcol"),
    )
    out_specs = (P("pcol", None), P("pcol", None), P(("prow", "pcol"), None))
    return jax.shard_map(local, mesh=mesh, in_specs=in_specs, out_specs=out_specs, check_vma=False)
```

profile of v0, /device:TPU:1, one launch (start us, length us, event | category | flops | bytes accessed | tf_op | source)
XLA Modules:
  0.0 624.2 jit_solution(3080631733843241181)
XLA Ops:
  7.2 2.1 fusion.3
  9.4 0.0 all-reduce.6.cloned.1.call-start
  9.4 179.8 %all-reduce.4.cloned.1.call-done = f32[512,256]{1,0:T(8,128)} async-done(((f32[512,256]{1,0:T(8,128)}), f32[512,256]{1,0:T(8,128)}) %all-reduce.4.cloned.1.call-update) | async-done | bytes 524304 | tf_op jit(solution)/shard_map/psum | solution.py:11
  189.2 2.0 convolution_bitcast_fusion.3
  191.2 0.0 all-reduce.8.cloned.1.call-start
  191.2 120.2 %all-reduce.6.cloned.1.call-done = f32[128,256]{1,0:T(8,128)} async-done(((f32[128,256]{1,0:T(8,128)}), f32[128,256]{1,0:T(8,128)}) %all-reduce.6.cloned.1.call-update) | async-done | bytes 131088 | tf_op jit(solution)/shard_map/psum | solution.py:27
  311.5 2.0 convolution_bitcast_fusion.2
  313.5 0.0 reduce-scatter.7.cloned.1.call-start
  313.5 0.6 convolution_bitcast_fusion.1
  314.2 1.5 copy.17
  315.7 0.0 reduce-scatter.9.cloned.1.call-start
  315.8 166.0 %all-reduce.8.cloned.1.call-done = f32[512,256]{0,1:T(8,128)} async-done(((f32[512,256]{0,1:T(8,128)}), f32[512,256]{0,1:T(8,128)}) %all-reduce.8.cloned.1.call-update) | async-done | bytes 524304 | tf_op jit(solution)/shard_map/psum | solution.py:11
  481.8 2.1 convolution_bitcast_fusion
  483.9 1.6 copy.19
  485.5 0.9 copy-done.5
  486.4 0.1 copy.14
  486.4 0.1 copy-done.2
  486.6 1.0 copy.15
  487.6 61.3 %reduce-scatter.7.cloned.1.call-done = f32[88,256]{1,0:T(8,128)} async-done(((f32[1408,256]{1,0:T(8,128)}), f32[88,256]{1,0:T(8,128)}) %reduce-scatter.7.cloned.1.call-update) | async-done | bytes 90128
  548.8 1.0 copy.18
  549.8 65.4 %reduce-scatter.9.cloned.1.call-done = f32[88,256]{1,0:T(8,128)} async-done(((f32[1408,256]{1,0:T(8,128)}), f32[88,256]{1,0:T(8,128)}) %reduce-scatter.9.cloned.1.call-update) | async-done | bytes 90128
  615.2 1.0 copy.20
  616.2 0.7 copy.16
  616.9 0.8 copy.24
  (17 shorter events, 0.2 us)
Async XLA Ops:
  7.2 306.3 %copy-start = (bf16[1408,512]{1,0:T(8,128)(2,1)S(1)}, bf16[1408,512]{1,0:T(8,128)(2,1)}, u32[]{:S(2)}) copy-start(bf16[1408,512]{1,0:T(8,128)(2,1)} %param.14) | copy-start | bytes 4325380
  7.2 304.3 %copy-start.3 = (bf16[512,128]{1,0:T(8,128)(2,1)S(1)}, bf16[512,128]{1,0:T(8,128)(2,1)}, u32[]{:S(2)}) copy-start(bf16[512,128]{1,0:T(8,128)(2,1)} %param.12) | copy-start | bytes 393220
  7.2 304.3 %copy-start.4 = (f32[128,256]{1,0:T(8,128)S(1)}, f32[128,256]{1,0:T(8,128)}, u32[]{:S(2)}) copy-start(f32[128,256]{1,0:T(8,128)} %param.9) | copy-start | bytes 393220
  7.2 182.0 %all-reduce.4.cloned.1.call-start = ((), (), s32[]{:S(2)}) async-start(), calls=%async_computation.2 | async-start | bytes 1048576 | tf_op jit(solution)/shard_map/psum | solution.py:11
  9.4 302.1 %all-reduce.6.cloned.1.call-start = ((), (), s32[]{:S(2)}) async-start(), calls=%async_computation.3 | async-start | bytes 262144 | tf_op jit(solution)/shard_map/psum | solution.py:27
  189.2 124.4 %copy-start.1 = (f32[512,256]{1,0:T(8,128)S(1)}, f32[512,256]{1,0:T(8,128)}, u32[]{:S(2)}) copy-start(f32[512,256]{1,0:T(8,128)} %all-reduce.4.cloned.1.call-done) | copy-start | bytes 1572868
  191.2 290.6 %all-reduce.8.cloned.1.call-start = ((), (), s32[]{:S(2)}) async-start(), calls=%async_computation.4 | async-start | bytes 1048576 | tf_op jit(solution)/shard_map/psum | solution.py:11
  313.5 235.4 %reduce-scatter.7.cloned.1.call-start = ((), (), s32[]{:S(2)}) async-start(), calls=%async_computation.5 | async-start | bytes 1531904
  315.7 299.5 %reduce-scatter.9.cloned.1.call-start = ((), (), s32[]{:S(2)}) async-start(), calls=%async_computation.6 | async-start | bytes 1531904
  485.5 0.9 copy-start.5
  485.5 1.1 copy-start.2
Sparse Core Ops, SparseCore 0:
  11.8 177.2 all-reduce.3
  192.1 119.2 all-reduce.5
  315.3 166.4 all-reduce.7
  485.4 63.3 reduce-scatter.6
  552.5 62.6 reduce-scatter.8
where the time goes:
time: 625 us; the launch traced here: 624 us
  waiting for transfers between devices  593 us (95%)
  between operations  13.9 us (2%)
  matrix products  8.79 us (1%)
  local copies, waits for them, and re-layouts  8.64 us (1%)
    psum x2, waiting for transfers between devices, solve_block(): return lax.psum(partial_value, 'prow')  346 us
    unnamed x7, waiting for transfers between devices  127 us
    psum x1, waiting for transfers between devices, local(): second_rows = rhs_second - lax.psum(crossing, 'pcol')  120 us
  transfers between devices with their start and end apart: 5, of which 5 were waited for; matrix products, arithmetic and copies ran while one was open for 1% of the time, Pallas kernels for 0%

commit v1 on v0

v1 whole, which is shorter than its diff:
```python
import jax
import jax.numpy as jnp
from jax import lax
from jax.experimental import pallas as pl
from jax.experimental.pallas import tpu as pltpu
from jax.sharding import PartitionSpec as P

MESH = pl.DeviceIdType.MESH
F32 = jnp.float32
BF16 = jnp.bfloat16
NX = 8
FAR_FIRST = (4, 3, 5, 2, 6, 1, 7)


def kernel(
    r1_hbm, r2_hbm, rest_hbm, inv1_hbm, inv2_hbm, cross_hbm, pf_hbm, ps_hbm,
    o1_hbm, o2_hbm, o3_hbm,
    r1, r2, rest, inv1, inv2, cross, pf, ps,
    part, rs1, mid, rs2, full, rounded,
    cpart, cin, csum, yrs, sec,
    acc, pin, psum, yrs3, out,
    load_sem, store_sem, send_sem, recv_sem, pin_sem,
):
    r = lax.axis_index("prow")
    p = lax.axis_index("pcol")
    x, z = r // NX, r % NX
    y, c = p // 2, p % 2

    def at_x(k):
        return (lax.rem(x + k, NX) * NX + z, p)

    def at_z(k):
        return (x * NX + lax.rem(z + k, NX), p)

    def at_y(k):
        return (r, lax.rem(y + k, NX) * 2 + c)

    partner = (r, y * 2 + (1 - c))
    line = (at_x, at_z)

    loads = []
    for i, (src, dst) in enumerate(
        ((inv1_hbm, inv1), (r1_hbm, r1), (cross_hbm, cross), (r2_hbm, r2),
         (inv2_hbm, inv2), (pf_hbm, pf), (ps_hbm, ps), (rest_hbm, rest))
    ):
        cp = pltpu.make_async_copy(src, dst, load_sem.at[i])
        cp.start()
        loads.append(cp)

    barrier = pltpu.get_barrier_semaphore()
    for k in range(1, NX):
        for to in (at_x, at_z, at_y):
            pl.semaphore_signal(barrier, inc=1, device_id=to(k), device_id_type=MESH)
    pl.semaphore_signal(barrier, inc=1, device_id=partner, device_id_type=MESH)

    sent = []

    def send(src, dst, group, device, recv=None):
        pltpu.make_async_remote_copy(
            src_ref=src,
            dst_ref=dst,
            send_sem=send_sem.at[group],
            recv_sem=recv_sem.at[group] if recv is None else recv,
            device_id=device,
            device_id_type=MESH,
        ).start()

    def wait_bytes(ref, sem):
        pltpu.make_async_copy(ref, ref, sem).wait()

    def arrived(ref, group):
        wait_bytes(ref, recv_sem.at[group])
        sent.append((ref, group))

    loads[0].wait()
    loads[1].wait()

    def solve(b, inverse, values, after_first_sends=None):
        base = 8 * b
        total = jnp.dot(inverse[...], values.astype(BF16), preferred_element_type=F32)
        part[b, 0] = total[:, :128]
        part[b, 1] = total[:, 128:]
        if b == 0:
            pl.semaphore_wait(barrier, 3 * (NX - 1) + 1)
        mine = (x, z)
        for k in FAR_FIRST:
            for h in range(2):
                to = lax.rem(mine[h] + k, NX)
                send(part.at[b, h, pl.ds(pl.multiple_of(to * 64, 64), 64)], rs1.at[b, h, k - 1], base + h, line[h](k))
        if after_first_sends is not None:
            after_first_sends()
        for h in range(2):
            arrived(rs1.at[b, h], base + h)
            s = part[b, h, pl.ds(pl.multiple_of(mine[h] * 64, 64), 64)]
            for k in range(1, NX):
                s = s + rs1[b, h, k - 1]
            mid[b, h] = s
            other = mine[1 - h]
            for k in FAR_FIRST:
                to = lax.rem(other + k, NX)
                send(mid.at[b, h, pl.ds(pl.multiple_of(to * 8, 8), 8)], rs2.at[b, h, k - 1], base + 2 + h, line[1 - h](k))
        for h in range(2):
            other = mine[1 - h]
            arrived(rs2.at[b, h], base + 2 + h)
            s = mid[b, h, pl.ds(pl.multiple_of(other * 8, 8), 8)]
            for k in range(1, NX):
                s = s + rs2[b, h, k - 1]
            row = pl.multiple_of(mine[h] * 64 + other * 8, 8)
            full[b, h, pl.ds(row, 8)] = s
            for k in FAR_FIRST:
                here = full.at[b, h, pl.ds(row, 8)]
                send(here, here, base + 4 + h, line[1 - h](k))
        for h in range(2):
            arrived(full.at[b, h, pl.ds(0, 56)], base + 4 + h)
            for k in FAR_FIRST:
                here = full.at[b, h, pl.ds(pl.multiple_of(mine[h] * 64, 64), 64)]
                send(here, here, base + 6 + h, line[h](k))
        for h in range(2):
            arrived(full.at[b, h, pl.ds(0, 448)], base + 6 + h)
            rounded[b, :, h * 128 : (h + 1) * 128] = full[b, h].astype(BF16)

    def store(b, out_hbm):
        cps = []
        for h in range(2):
            cp = pltpu.make_async_copy(full.at[b, h], out_hbm.at[:, pl.ds(h * 128, 128)], store_sem.at[2 * b + h])
            cp.start()
            cps.append(cp)
        return cps

    solve(0, inv1, r1[...])

    g = 16
    loads[2].wait()
    cpart[...] = jnp.dot(cross[...], rounded[0], preferred_element_type=F32)
    send(cpart.at[pl.ds(pl.multiple_of((1 - c) * 64, 64), 64)], cin, g, partner)
    arrived(cin, g)
    csum[...] = cpart[pl.ds(pl.multiple_of(c * 64, 64), 64)] + cin[...]
    for k in FAR_FIRST:
        to = lax.rem(y + k, NX)
        send(csum.at[pl.ds(pl.multiple_of(to * 8, 8), 8)], yrs.at[k - 1], g + 1, at_y(k))
    stores = store(0, o1_hbm)
    loads[3].wait()
    loads[4].wait()
    loads[5].wait()

    def first_update(i, carry):
        acc[i] = jnp.dot(
            pf[pl.ds(pl.multiple_of(i * 176, 176), 176)], rounded[0], preferred_element_type=F32
        ).reshape(2, 88, 256)
        return carry

    lax.fori_loop(0, NX, first_update, 0)
    arrived(yrs, g + 1)
    s = csum[pl.ds(pl.multiple_of(y * 8, 8), 8)]
    for k in range(1, NX):
        s = s + yrs[k - 1]
    row = pl.multiple_of(c * 64 + y * 8, 8)
    sec[pl.ds(row, 8)] = r2[pl.ds(row, 8)] - s
    for k in FAR_FIRST:
        here = sec.at[pl.ds(row, 8)]
        send(here, here, g + 2, at_y(k))
    arrived(sec.at[pl.ds(0, 56)], g + 2)
    here = sec.at[pl.ds(pl.multiple_of(c * 64, 64), 64)]
    send(here, here, g + 3, partner)
    arrived(sec.at[pl.ds(0, 64)], g + 3)

    solve(1, inv2, sec[...])

    loads[6].wait()
    for k in FAR_FIRST + (0,):
        to = lax.rem(y + k, NX)
        acc[to] = acc[to] + jnp.dot(
            ps[pl.ds(pl.multiple_of(to * 176, 176), 176)], rounded[1], preferred_element_type=F32
        ).reshape(2, 88, 256)
        send(acc.at[to, 1 - c], pin.at[k], g + 4, partner, pin_sem.at[k])
    stores += store(1, o2_hbm)
    for k in FAR_FIRST:
        to = lax.rem(y + k, NX)
        wait_bytes(pin.at[k], pin_sem.at[k])
        psum[k] = acc[to, c] + pin[k]
        send(psum.at[k], yrs3.at[k - 1], g + 5, at_y(k))
    wait_bytes(pin.at[0], pin_sem.at[0])
    loads[7].wait()
    s = acc[y, c] + pin[0]
    arrived(yrs3, g + 5)
    for k in range(1, NX):
        s = s + yrs3[k - 1]
    out[...] = rest[...] - s
    cp = pltpu.make_async_copy(out, o3_hbm, store_sem.at[4])
    cp.start()
    stores.append(cp)
    for ref, group in sent:
        wait_bytes(ref, send_sem.at[group])
    wait_bytes(pin, send_sem.at[g + 4])
    for cp in stores:
        cp.wait()


def solution(mesh):
    def local(rhs_first, rhs_second, rhs_rest, inverse_first, inverse_second, panel_cross, panel_first, panel_second):
        any_spec = pl.BlockSpec(memory_space=pltpu.HBM)
        arguments = (rhs_first, rhs_second, rhs_rest, inverse_first, inverse_second, panel_cross, panel_first, panel_second)
        return pl.pallas_call(
            kernel,
            out_shape=(
                jax.ShapeDtypeStruct((512, 256), F32),
                jax.ShapeDtypeStruct((512, 256), F32),
                jax.ShapeDtypeStruct((88, 256), F32),
            ),
            in_specs=[any_spec] * 8,
            out_specs=(any_spec,) * 3,
            scratch_shapes=[pltpu.VMEM(a.shape, a.dtype) for a in arguments]
            + [
                pltpu.VMEM((2, 2, 512, 128), F32),
                pltpu.VMEM((2, 2, 7, 64, 128), F32),
                pltpu.VMEM((2, 2, 64, 128), F32),
                pltpu.VMEM((2, 2, 7, 8, 128), F32),
                pltpu.VMEM((2, 2, 512, 128), F32),
                pltpu.VMEM((2, 512, 256), BF16),
                pltpu.VMEM((128, 256), F32),
                pltpu.VMEM((64, 256), F32),
                pltpu.VMEM((64, 256), F32),
                pltpu.VMEM((7, 8, 256), F32),
                pltpu.VMEM((128, 256), F32),
                pltpu.VMEM((8, 2, 88, 256), F32),
                pltpu.VMEM((8, 88, 256), F32),
                pltpu.VMEM((8, 88, 256), F32),
                pltpu.VMEM((7, 88, 256), F32),
                pltpu.VMEM((88, 256), F32),
                pltpu.SemaphoreType.DMA((8,)),
                pltpu.SemaphoreType.DMA((5,)),
                pltpu.SemaphoreType.DMA((24,)),
                pltpu.SemaphoreType.DMA((24,)),
                pltpu.SemaphoreType.DMA((8,)),
            ],
            compiler_params=pltpu.CompilerParams(
                collective_id=0, has_side_effects=True, vmem_limit_bytes=60 * 2**20
            ),
            cost_estimate=pl.CostEstimate(flops=10**9, bytes_accessed=5 * 10**6, transcendentals=0),
        )(*arguments)

    in_specs = (
        P("prow", None),
        P("prow", None),
        P(("prow", "pcol"), None),
        P("pcol", "prow"),
        P("pcol", "prow"),
        P("prow", "pcol"),
        P("prow", "pcol"),
        P("prow", "pcol"),
    )
    out_specs = (P("pcol", None), P("pcol", None), P(("prow", "pcol"), None))
    return jax.shard_map(local, mesh=mesh, in_specs=in_specs, out_specs=out_specs, check_vma=False)
```

time: 625 us -> 107 us (0.17)
  waiting for transfers between devices: 593 us -> 0 us
  Pallas kernels: 0 us -> 102 us
  between operations: 13.9 us -> 0.65 us
  matrix products: 8.79 us -> 0 us
    psum x3 -> x0, waiting for transfers between devices: 466 us -> none  [the longest x2 346 us: solve_block(): return lax.psum(partial_value, 'prow')]
    unnamed x7 -> x0, waiting for transfers between devices: 127 us -> none
    pallas_call x0 -> x1, Pallas kernels: none -> 102 us  [local(): pl.pallas_call(kernel, out_shape=(jax.ShapeDtypeStruct((512, 256), F32),...]
    dot_general x5 -> x0, matrix products: 8.79 us -> none  [the longest x2 4.04 us: solve_block(): jnp.dot(inverse_local, block_values.astype(jnp.bfloat16), preferred_eleme...]
  transfers between devices with their start and end apart: 5 -> 0, of which waited for: 5 -> 0; matrix products, arithmetic and copies ran while one was open for 1% -> 0% of each run, Pallas kernels for 0% -> 0%
where the time goes in v1:
time: 107 us
  Pallas kernels  102 us (95%)
  local copies, waits for them, and re-layouts  4.41 us (4%)
    pallas_call x1, Pallas kernels, local(): pl.pallas_call(kernel, out_shape=(jax.ShapeDtypeStruct((512, 256), F32),...  102 us
    unnamed x5, local copies, waits for them, and re-layouts  4.41 us

profile of v1, /device:TPU:1, one launch (start us, length us, event | category | flops | bytes accessed | tf_op | source)
XLA Modules:
  0.0 107.0 jit_solution(5229918573847307871)
XLA Ops:
  0.6 102.0 %shard_map.103 = (f32[512,256]{1,0:T(8,128)}, f32[512,256]{1,0:T(8,128)}, f32[88,256]{1,0:T(8,128)}) custom-call(f32[128,256]{1,0:T(8,128)} %r1_hbm.1, f32[128,256]{1,0:T(8,128)} %r2_hbm.1, f32[88,256]{1,0:T(8,128)} %rest_hbm.1, bf16[512,128]{1,0:T(8,128)(2,1)} %inv1_hbm.1, bf16[512,128]{1,0:T(8,128)(2,1)} %inv2_hbm.1, bf16[128,512]{1,0:T(8,128)(2,1)} %cross_hbm.1, ...), custom_call_target="tpu_custom_call" | custom-call | flops 1000000000 | bytes 5000000 | tf_op jit(solution)/shard_map/pallas_call | solution.py:203
  102.6 0.0 copy-start
  102.6 1.9 %copy.14 = f32[512,256]{1,0:T(8,128)} copy(f32[512,256]{1,0:T(8,128)} %get-tuple-element.6) | data formatting | bytes 1048576
  104.5 1.9 %copy.15 = f32[512,256]{1,0:T(8,128)} copy(f32[512,256]{1,0:T(8,128)} %get-tuple-element.7) | data formatting | bytes 1048576
  106.4 0.0 copy-done
  106.4 0.6 copy.16
Async XLA Ops:
  102.6 3.8 %copy-start = (f32[88,256]{1,0:T(8,128)S(1)}, f32[88,256]{1,0:T(8,128)}, u32[]{:S(2)}) copy-start(f32[88,256]{1,0:T(8,128)} %get-tuple-element.8) | copy-start | bytes 270340

commit v2 on v0

v2 whole, which is shorter than its diff:
```python
import jax
import jax.numpy as jnp
from jax import lax
from jax.experimental import pallas as pl
from jax.experimental.pallas import tpu as pltpu
from jax.sharding import PartitionSpec as P

MESH = pl.DeviceIdType.MESH
F32 = jnp.float32
BF16 = jnp.bfloat16
NX = 8
FAR_FIRST = (4, 3, 5, 2, 6, 1, 7)
N_GROUPS = 44
PIECES = (pl.ds(0, 48), pl.ds(48, 40))


def kernel(
    r1_hbm, r2_hbm, rest_hbm, inv1_hbm, inv2_hbm, cross_hbm, pf_hbm, ps_hbm,
    o1_hbm, o2_hbm, o3_hbm,
    r1, r2, rest, inv1, inv2, cross, pf, ps,
    part, rs1, mid, rs2, full, rounded,
    cpart, yrs, sec,
    acc, pin, ring_in, ring_out, out,
    load_sem, store_sem, send_sem, recv_sem, pin_sem, ring_sem,
):
    r = lax.axis_index("prow")
    p = lax.axis_index("pcol")
    x, z = r // NX, r % NX
    y, c = p // 2, p % 2
    mine = (x, z)

    def at_x(k):
        return (lax.rem(x + k, NX) * NX + z, p)

    def at_z(k):
        return (x * NX + lax.rem(z + k, NX), p)

    def at_y(k, other_core=0):
        return (r, lax.rem(y + k, NX) * 2 + (1 - c if other_core else c))

    partner = at_y(0, 1)
    column = [(k, f) for k in FAR_FIRST for f in range(2)] + [(0, 1)]
    line = (at_x, at_z)

    def rows(start, count):
        return pl.ds(pl.multiple_of(start, 8), count)

    loads = []
    for i, (src, dst) in enumerate(
        ((inv1_hbm, inv1), (r1_hbm, r1), (cross_hbm, cross), (r2_hbm, r2),
         (inv2_hbm, inv2), (pf_hbm, pf), (ps_hbm, ps), (rest_hbm, rest))
    ):
        cp = pltpu.make_async_copy(src, dst, load_sem.at[i])
        cp.start()
        loads.append(cp)

    barrier = pltpu.get_barrier_semaphore()
    for k in range(1, NX):
        for to in line:
            pl.semaphore_signal(barrier, inc=1, device_id=to(k), device_id_type=MESH)
    for k, f in column:
        pl.semaphore_signal(barrier, inc=1, device_id=at_y(k, f), device_id_type=MESH)

    def send(src, dst, group, device, recv=None):
        pltpu.make_async_remote_copy(
            src_ref=src,
            dst_ref=dst,
            send_sem=send_sem.at[group],
            recv_sem=recv_sem.at[group] if recv is None else recv,
            device_id=device,
            device_id_type=MESH,
        ).start()

    def wait_bytes(ref, sem):
        pltpu.make_async_copy(ref, ref, sem).wait()

    at_end = []
    stores = []

    def arrived(ref, group):
        wait_bytes(ref, recv_sem.at[group])
        at_end.append(lambda: wait_bytes(ref, send_sem.at[group]))

    def on_owner(h, s, yes, no):
        owner = lax.rem(mine[1 - h], 2) == s
        pl.when(owner)(yes)
        if no is not None:
            pl.when(jnp.logical_not(owner))(no)

    def solve(b, s):
        def group(stage, h):
            return ((b * 2 + s) * 4 + stage) * 2 + h

        if s == 1:
            for h in range(2):
                wait_bytes(rs1.at[b, 0, h], send_sem.at[(b * 16 + 0) + h])
        for k in FAR_FIRST:
            for h in range(2):
                to = lax.rem(mine[h] + k, NX)
                send(part.at[b, s, rows(h * 256 + to * 32, 32)], rs1.at[b, s, h, k - 1], group(0, h), line[h](k))
        yield
        for h in range(2):
            if s == 1:
                arrived(rs1.at[b, s, h], group(0, h))
            else:
                wait_bytes(rs1.at[b, s, h], recv_sem.at[group(0, h)])
            value = part[b, s, rows(h * 256 + mine[h] * 32, 32)]
            for k in range(1, NX):
                value = value + rs1[b, s, h, k - 1]
            mid[b, s, h] = value
            other = mine[1 - h]

            def spread(ks, h=h, other=other):
                for k in ks:
                    to = lax.rem(other + k, NX)
                    send(mid.at[b, s, h, rows(to // 2 * 8, 8)], rs2.at[b, s, h, k - 1], group(1, h), line[1 - h](k))

            on_owner(h, s, lambda: spread((4, 2, 6)), lambda: spread((3, 5, 1, 7)))
        yield
        for h in range(2):
            other = mine[1 - h]

            def finish(h=h, other=other):
                wait_bytes(rs2.at[b, s, h], recv_sem.at[group(1, h)])
                value = mid[b, s, h, rows(other // 2 * 8, 8)]
                for k in range(1, NX):
                    value = value + rs2[b, s, h, k - 1]
                place = rows(h * 256 + mine[h] * 32 + other // 2 * 8, 8)
                full[b, s, place] = value
                here = full.at[b, s, place]
                for k in FAR_FIRST:
                    send(here, here, group(2, h), line[1 - h](k))

            on_owner(h, s, finish, None)
        yield
        for h in range(2):

            def gathered(count, h=h):
                wait_bytes(full.at[b, s, pl.ds(0, count)], recv_sem.at[group(2, h)])

            on_owner(h, s, lambda: gathered(24), lambda: gathered(32))
            here = full.at[b, s, rows(h * 256 + mine[h] * 32, 32)]
            for k in FAR_FIRST:
                send(here, here, group(3, h), line[h](k))

            def leave(owner, h=h):
                wait_bytes(mid.at[b, s, h, pl.ds(0, 24 if owner else 32)], send_sem.at[group(1, h)])
                if owner:
                    wait_bytes(full.at[b, s, pl.ds(0, 56)], send_sem.at[group(2, h)])

            at_end.append(lambda h=h, leave=leave: on_owner(h, s, lambda: leave(True), lambda: leave(False)))
        yield
        for h in range(2):
            arrived(full.at[b, s, pl.ds(0, 224)], group(3, h))
        rounded[b, :, s * 128 : (s + 1) * 128] = full[b, s].astype(BF16)

    def store(b, s, out_hbm):
        cp = pltpu.make_async_copy(full.at[b, s], out_hbm.at[:, pl.ds(s * 128, 128)], store_sem.at[2 * b + s])
        cp.start()
        stores.append(cp)

    def first_update(i, carry):
        update = jnp.dot(pf[pl.ds(pl.multiple_of(i * 176, 176), 176)], rounded[0], preferred_element_type=F32)
        for core in range(2):
            for h in range(2):
                acc[i, core, h] = update[core * 88 : (core + 1) * 88, h * 128 : (h + 1) * 128]
        return carry

    up, down = at_y(1), at_y(NX - 1)

    def stream(s):
        columns = slice(s * 128, (s + 1) * 128)
        yield from solve(0, s)

        g = 32 + 4 * s
        if s == 0:
            loads[2].wait()
        cpart[s] = jnp.dot(cross[...], rounded[0, :, columns], preferred_element_type=F32)
        for k, f in column:
            to = at_y(k, f)
            send(cpart.at[s, rows(to[1] * 8, 8)], yrs.at[s, 2 * k + f - 1], g, to)
        store(0, s, o1_hbm)
        if s == 1:
            loads[5].wait()
            lax.fori_loop(0, 2, first_update, 0)
        yield
        if s == 0:
            loads[3].wait()
        arrived(yrs.at[s], g)
        place = rows(p * 8, 8)
        value = cpart[s, place]
        for i in range(15):
            value = value + yrs[s, i]
        sec[s, place] = r2[place, columns] - value
        here = sec.at[s, place]
        for k, f in column:
            send(here, here, g + 1, at_y(k, f))
        if s == 1:
            lax.fori_loop(2, 4, first_update, 0)
        yield
        if s == 0:
            loads[4].wait()
        arrived(sec.at[s, pl.ds(0, 120)], g + 1)
        part[1, s] = jnp.dot(inv2[...], sec[s].astype(BF16), preferred_element_type=F32)
        solving = solve(1, s)
        next(solving)
        if s == 1:
            lax.fori_loop(4, 8, first_update, 0)
        yield
        yield from solving

        store(1, s, o2_hbm)
        if s == 0:
            loads[6].wait()

        def second_update(ks):
            for k in ks:
                to = lax.rem(y + k, NX)
                update = jnp.dot(ps[pl.ds(pl.multiple_of(to * 176, 176), 176)], rounded[1, :, columns], preferred_element_type=F32)
                for core in range(2):
                    acc[to, core, s] += update[core * 88 : (core + 1) * 88]
                send(acc.at[to, 1 - c, s], pin.at[k, s], 40 + s, partner, pin_sem.at[k, s])

        ready = set()

        def summed(k, part_rows):
            if k not in ready:
                wait_bytes(pin.at[k, s], pin_sem.at[k, s])
                ready.add(k)
            return acc[lax.rem(y + k, NX), c, s, part_rows] + pin[k, s, part_rows]

        slots = iter(range(7))

        def pass_on(step, way):
            slot = next(slots)
            for i, part_rows in enumerate(PIECES):
                value = summed(5 - step if way == 0 else NX - (5 - step), part_rows)
                if step > (1 if way == s else 2):
                    come = ring_in.at[way, step - 2, s, part_rows]
                    wait_bytes(come, ring_sem.at[way, step - 2, s, i])
                    value = value + come[...]
                ring_out[s, slot, part_rows] = value
                send(
                    ring_out.at[s, slot, part_rows], ring_in.at[way, step - 1, s, part_rows], 42 + s,
                    (up, down)[way], ring_sem.at[way, step - 1, s, i],
                )

        second_update((4, 3, 5, 2) if s == 0 else (4, 5, 3, 6))
        pass_on(1, s)
        pass_on(2, 1 - s)
        second_update((6, 1, 7, 0) if s == 0 else (2, 7, 1, 0))
        yield
        pass_on(2, s)
        yield
        pass_on(3, 1 - s)
        pass_on(3, s)
        yield
        pass_on(4, 1 - s)
        pass_on(4, s)
        yield
        if s == 0:
            loads[7].wait()
        for i, part_rows in enumerate(PIECES):
            value = summed(0, part_rows)
            for way in range(2):
                come = ring_in.at[way, 3, s, part_rows]
                wait_bytes(come, ring_sem.at[way, 3, s, i])
                value = value + come[...]
            out[s, part_rows] = rest[part_rows, columns] - value
        cp = pltpu.make_async_copy(out.at[s], o3_hbm.at[:, pl.ds(s * 128, 128)], store_sem.at[4 + s])
        cp.start()
        stores.append(cp)
        at_end.append(lambda: wait_bytes(pin.at[:, s], send_sem.at[40 + s]))
        at_end.append(lambda: wait_bytes(ring_out.at[s], send_sem.at[42 + s]))

    loads[0].wait()
    loads[1].wait()
    total = jnp.dot(inv1[...], r1[...].astype(BF16), preferred_element_type=F32)
    part[0, 0] = total[:, :128]
    part[0, 1] = total[:, 128:]
    pl.semaphore_wait(barrier, 2 * (NX - 1) + len(column))
    streams = [stream(0), stream(1)]
    while streams:
        for one in list(streams):
            try:
                next(one)
            except StopIteration:
                streams.remove(one)
    for end in at_end:
        end()
    for cp in stores:
        cp.wait()


def copy_kernel(a1, a2, a3, b1, b2, b3, v1, v2, v3, in_sem, out_sem):
    pieces = [(a3, v3, b3)]
    for i in range(4):
        rows = pl.ds(i * 128, 128)
        pieces += [(a1.at[rows], v1.at[rows], b1.at[rows]), (a2.at[rows], v2.at[rows], b2.at[rows])]
    come = [pltpu.make_async_copy(a, v, in_sem.at[i]) for i, (a, v, b) in enumerate(pieces)]
    go = [pltpu.make_async_copy(v, b, out_sem.at[i]) for i, (a, v, b) in enumerate(pieces)]
    for cp in come:
        cp.start()
    for cp, then in zip(come, go):
        cp.wait()
        then.start()
    for cp in go:
        cp.wait()


def solution(mesh):
    def local(rhs_first, rhs_second, rhs_rest, inverse_first, inverse_second, panel_cross, panel_first, panel_second):
        any_spec = pl.BlockSpec(memory_space=pltpu.HBM)
        arguments = (rhs_first, rhs_second, rhs_rest, inverse_first, inverse_second, panel_cross, panel_first, panel_second)
        shapes = (
            jax.ShapeDtypeStruct((512, 256), F32),
            jax.ShapeDtypeStruct((512, 256), F32),
            jax.ShapeDtypeStruct((88, 256), F32),
        )
        results = pl.pallas_call(
            kernel,
            out_shape=shapes,
            in_specs=[any_spec] * 8,
            out_specs=(any_spec,) * 3,
            scratch_shapes=[pltpu.VMEM(a.shape, a.dtype) for a in arguments]
            + [
                pltpu.VMEM((2, 2, 512, 128), F32),
                pltpu.VMEM((2, 2, 2, 7, 32, 128), F32),
                pltpu.VMEM((2, 2, 2, 32, 128), F32),
                pltpu.VMEM((2, 2, 2, 7, 8, 128), F32),
                pltpu.VMEM((2, 2, 512, 128), F32),
                pltpu.VMEM((2, 512, 256), BF16),
                pltpu.VMEM((2, 128, 128), F32),
                pltpu.VMEM((2, 15, 8, 128), F32),
                pltpu.VMEM((2, 128, 128), F32),
                pltpu.VMEM((8, 2, 2, 88, 128), F32),
                pltpu.VMEM((8, 2, 88, 128), F32),
                pltpu.VMEM((2, 4, 2, 88, 128), F32),
                pltpu.VMEM((2, 7, 88, 128), F32),
                pltpu.VMEM((2, 88, 128), F32),
                pltpu.SemaphoreType.DMA((8,)),
                pltpu.SemaphoreType.DMA((6,)),
                pltpu.SemaphoreType.DMA((N_GROUPS,)),
                pltpu.SemaphoreType.DMA((N_GROUPS,)),
                pltpu.SemaphoreType.DMA((8, 2)),
                pltpu.SemaphoreType.DMA((2, 4, 2, len(PIECES))),
            ],
            compiler_params=pltpu.CompilerParams(
                collective_id=0, has_side_effects=True, vmem_limit_bytes=60 * 2**20
            ),
            cost_estimate=pl.CostEstimate(flops=10**9, bytes_accessed=5 * 10**6, transcendentals=0),
        )(*arguments)
        return pl.pallas_call(
            copy_kernel,
            out_shape=shapes,
            in_specs=[any_spec] * 3,
            out_specs=(any_spec,) * 3,
            scratch_shapes=[pltpu.VMEM(a.shape, a.dtype) for a in shapes]
            + [pltpu.SemaphoreType.DMA((9,)), pltpu.SemaphoreType.DMA((9,))],
            compiler_params=pltpu.CompilerParams(vmem_limit_bytes=60 * 2**20),
        )(*results)

    in_specs = (
        P("prow", None),
        P("prow", None),
        P(("prow", "pcol"), None),
        P("pcol", "prow"),
        P("pcol", "prow"),
        P("prow", "pcol"),
        P("prow", "pcol"),
        P("prow", "pcol"),
    )
    out_specs = (P("pcol", None), P("pcol", None), P(("prow", "pcol"), None))
    return jax.shard_map(local, mesh=mesh, in_specs=in_specs, out_specs=out_specs, check_vma=False)
```

time: 625 us -> 93.9 us (0.15)
  waiting for transfers between devices: 593 us -> 0 us
  Pallas kernels: 0 us -> 91.6 us
  between operations: 13.9 us -> 0.64 us
  matrix products: 8.79 us -> 0 us
  local copies, waits for them, and re-layouts: 8.64 us -> 0 us
    psum x3 -> x0, waiting for transfers between devices: 466 us -> none  [the longest x2 346 us: solve_block(): return lax.psum(partial_value, 'prow')]
    unnamed x7 -> x0, waiting for transfers between devices: 127 us -> none
    pallas_call x0 -> x2, Pallas kernels: none -> 91.6 us  [the longest x1 89.5 us: local(): pl.pallas_call(kernel, out_shape=shapes, in_specs=[any_spec] * 8, out_spe...]
    dot_general x5 -> x0, matrix products: 8.79 us -> none  [the longest x2 4.04 us: solve_block(): jnp.dot(inverse_local, block_values.astype(jnp.bfloat16), preferred_eleme...]
    unnamed x20 -> x0, local copies, waits for them, and re-layouts: 8.64 us -> none
  transfers between devices with their start and end apart: 5 -> 0, of which waited for: 5 -> 0; matrix products, arithmetic and copies ran while one was open for 1% -> 0% of each run, Pallas kernels for 0% -> 0%
where the time goes in v2:
time: 93.9 us; the launch traced here: 92.3 us
  Pallas kernels  91.6 us (98%)
    pallas_call x1, Pallas kernels, local(): pl.pallas_call(kernel, out_shape=shapes, in_specs=[any_spec] * 8, out_spe...  89.5 us
    pallas_call x1, Pallas kernels, local(): pl.pallas_call(copy_kernel, out_shape=shapes, in_specs=[any_spec] * 3, ou...  2.15 us

profile of v2, /device:TPU:1, one launch (start us, length us, event | category | flops | bytes accessed | tf_op | source)
XLA Modules:
  0.0 92.3 jit_solution(4447378896153118162)
XLA Ops:
  0.6 89.5 %shard_map.103 = (f32[512,256]{1,0:T(8,128)}, f32[512,256]{1,0:T(8,128)}, f32[88,256]{1,0:T(8,128)}) custom-call(f32[128,256]{1,0:T(8,128)} %r1_hbm.1, f32[128,256]{1,0:T(8,128)} %r2_hbm.1, f32[88,256]{1,0:T(8,128)} %rest_hbm.1, bf16[512,128]{1,0:T(8,128)(2,1)} %inv1_hbm.1, bf16[512,128]{1,0:T(8,128)(2,1)} %inv2_hbm.1, bf16[128,512]{1,0:T(8,128)(2,1)} %cross_hbm.1, ...), custom_call_target="tpu_custom_call" | custom-call | flops 1000000000 | bytes 5000000 | tf_op jit(solution)/shard_map/pallas_call | solution.py:320
  90.1 2.1 %shard_map.104 = (f32[512,256]{1,0:T(8,128)}, f32[512,256]{1,0:T(8,128)}, f32[88,256]{1,0:T(8,128)}) custom-call(f32[512,256]{1,0:T(8,128)} %get-tuple-element.6.a1, f32[512,256]{1,0:T(8,128)} %get-tuple-element.7.a2, f32[88,256]{1,0:T(8,128)} %get-tuple-element.8.a3), custom_call_target="tpu_custom_call" | custom-call | tf_op jit(solution)/shard_map/pallas_call | solution.py:353

commit v3 on v2

--- a/solution.py
+++ b/solution.py
@@ -81,12 +81,6 @@
         wait_bytes(ref, recv_sem.at[group])
         at_end.append(lambda: wait_bytes(ref, send_sem.at[group]))
 
-    def on_owner(h, s, yes, no):
-        owner = lax.rem(mine[1 - h], 2) == s
-        pl.when(owner)(yes)
-        if no is not None:
-            pl.when(jnp.logical_not(owner))(no)
-
     def solve(b, s):
         def group(stage, h):
             return ((b * 2 + s) * 4 + stage) * 2 + h
@@ -107,48 +101,22 @@
             value = part[b, s, rows(h * 256 + mine[h] * 32, 32)]
             for k in range(1, NX):
                 value = value + rs1[b, s, h, k - 1]
+            other = mine[1 - h]
             mid[b, s, h] = value
-            other = mine[1 - h]
-
-            def spread(ks, h=h, other=other):
-                for k in ks:
-                    to = lax.rem(other + k, NX)
-                    send(mid.at[b, s, h, rows(to // 2 * 8, 8)], rs2.at[b, s, h, k - 1], group(1, h), line[1 - h](k))
-
-            on_owner(h, s, lambda: spread((4, 2, 6)), lambda: spread((3, 5, 1, 7)))
+            rs2[b, s, h, other] = value
+            for k in FAR_FIRST:
+                send(mid.at[b, s, h], rs2.at[b, s, h, other], group(1, h), line[1 - h](k))
         yield
         for h in range(2):
-            other = mine[1 - h]
-
-            def finish(h=h, other=other):
-                wait_bytes(rs2.at[b, s, h], recv_sem.at[group(1, h)])
-                value = mid[b, s, h, rows(other // 2 * 8, 8)]
-                for k in range(1, NX):
-                    value = value + rs2[b, s, h, k - 1]
-                place = rows(h * 256 + mine[h] * 32 + other // 2 * 8, 8)
-                full[b, s, place] = value
-                here = full.at[b, s, place]
-                for k in FAR_FIRST:
-                    send(here, here, group(2, h), line[1 - h](k))
-
-            on_owner(h, s, finish, None)
-        yield
-        for h in range(2):
-
-            def gathered(count, h=h):
-                wait_bytes(full.at[b, s, pl.ds(0, count)], recv_sem.at[group(2, h)])
-
-            on_owner(h, s, lambda: gathered(24), lambda: gathered(32))
-            here = full.at[b, s, rows(h * 256 + mine[h] * 32, 32)]
+            arrived(rs2.at[b, s, h, pl.ds(0, 7)], group(1, h))
+            value = rs2[b, s, h, 0]
+            for i in range(1, NX):
+                value = value + rs2[b, s, h, i]
+            place = rows(h * 256 + mine[h] * 32, 32)
+            full[b, s, place] = value
+            here = full.at[b, s, place]
             for k in FAR_FIRST:
                 send(here, here, group(3, h), line[h](k))
-
-            def leave(owner, h=h):
-                wait_bytes(mid.at[b, s, h, pl.ds(0, 24 if owner else 32)], send_sem.at[group(1, h)])
-                if owner:
-                    wait_bytes(full.at[b, s, pl.ds(0, 56)], send_sem.at[group(2, h)])
-
-            at_end.append(lambda h=h, leave=leave: on_owner(h, s, lambda: leave(True), lambda: leave(False)))
         yield
         for h in range(2):
             arrived(full.at[b, s, pl.ds(0, 224)], group(3, h))
@@ -327,7 +295,7 @@
                 pltpu.VMEM((2, 2, 512, 128), F32),
                 pltpu.VMEM((2, 2, 2, 7, 32, 128), F32),
                 pltpu.VMEM((2, 2, 2, 32, 128), F32),
-                pltpu.VMEM((2, 2, 2, 7, 8, 128), F32),
+                pltpu.VMEM((2, 2, 2, 8, 32, 128), F32),
                 pltpu.VMEM((2, 2, 512, 128), F32),
                 pltpu.VMEM((2, 512, 256), BF16),
                 pltpu.VMEM((2, 128, 128), F32),

time: 93.9 us -> 89 us (0.948); the launches traced: 92.3 us -> 88.7 us
  Pallas kernels: 91.6 us -> 88 us
    pallas_call x1, Pallas kernels: 89.5 us -> 85.9 us  [local(): pl.pallas_call(kernel, out_shape=shapes, in_specs=[any_spec] * 8, out_spe...]
where the time goes in v3:
time: 89 us; the launch traced here: 88.7 us
  Pallas kernels  88 us (99%)
    pallas_call x1, Pallas kernels, local(): pl.pallas_call(kernel, out_shape=shapes, in_specs=[any_spec] * 8, out_spe...  85.9 us
    pallas_call x1, Pallas kernels, local(): pl.pallas_call(copy_kernel, out_shape=shapes, in_specs=[any_spec] * 3, ou...  2.15 us

profile of v3, /device:TPU:1, one launch (start us, length us, event | category | flops | bytes accessed | tf_op | source)
XLA Modules:
  0.0 88.7 jit_solution(6133069042312109774)
XLA Ops:
  0.6 85.9 %shard_map.103 = (f32[512,256]{1,0:T(8,128)}, f32[512,256]{1,0:T(8,128)}, f32[88,256]{1,0:T(8,128)}) custom-call(f32[128,256]{1,0:T(8,128)} %r1_hbm.1, f32[128,256]{1,0:T(8,128)} %r2_hbm.1, f32[88,256]{1,0:T(8,128)} %rest_hbm.1, bf16[512,128]{1,0:T(8,128)(2,1)} %inv1_hbm.1, bf16[512,128]{1,0:T(8,128)(2,1)} %inv2_hbm.1, bf16[128,512]{1,0:T(8,128)(2,1)} %cross_hbm.1, ...), custom_call_target="tpu_custom_call" | custom-call | flops 1000000000 | bytes 5000000 | tf_op jit(solution)/shard_map/pallas_call | solution.py:288
  86.5 2.1 %shard_map.104 = (f32[512,256]{1,0:T(8,128)}, f32[512,256]{1,0:T(8,128)}, f32[88,256]{1,0:T(8,128)}) custom-call(f32[512,256]{1,0:T(8,128)} %get-tuple-element.6.a1, f32[512,256]{1,0:T(8,128)} %get-tuple-element.7.a2, f32[88,256]{1,0:T(8,128)} %get-tuple-element.8.a3), custom_call_target="tpu_custom_call" | custom-call | tf_op jit(solution)/shard_map/pallas_call | solution.py:321

commit v4 on v3

--- a/solution.py
+++ b/solution.py
@@ -134,6 +134,10 @@
                 acc[i, core, h] = update[core * 88 : (core + 1) * 88, h * 128 : (h + 1) * 128]
         return carry
 
+    def first_updates(low, high):
+        for i in range(low, high):
+            first_update(i, 0)
+
     up, down = at_y(1), at_y(NX - 1)
 
     def stream(s):
@@ -150,7 +154,7 @@
         store(0, s, o1_hbm)
         if s == 1:
             loads[5].wait()
-            lax.fori_loop(0, 2, first_update, 0)
+            first_updates(0, 2)
         yield
         if s == 0:
             loads[3].wait()
@@ -164,7 +168,7 @@
         for k, f in column:
             send(here, here, g + 1, at_y(k, f))
         if s == 1:
-            lax.fori_loop(2, 4, first_update, 0)
+            first_updates(2, 4)
         yield
         if s == 0:
             loads[4].wait()
@@ -173,7 +177,7 @@
         solving = solve(1, s)
         next(solving)
         if s == 1:
-            lax.fori_loop(4, 8, first_update, 0)
+            first_updates(4, 8)
         yield
         yield from solving
 

time: 89 us -> 89 us (level)
  no operation moved by 1% of the time
where the time goes in v4:
time: 89 us; the launch traced here: 88.8 us
  Pallas kernels  88.1 us (99%)
    pallas_call x1, Pallas kernels, local(): pl.pallas_call(kernel, out_shape=shapes, in_specs=[any_spec] * 8, out_spe...  86 us
    pallas_call x1, Pallas kernels, local(): pl.pallas_call(copy_kernel, out_shape=shapes, in_specs=[any_spec] * 3, ou...  2.15 us

profile of v4, /device:TPU:1, one launch (start us, length us, event | category | flops | bytes accessed | tf_op | source)
XLA Modules:
  0.0 88.8 jit_solution(17066294673340362793)
XLA Ops:
  0.6 86.0 %shard_map.103 = (f32[512,256]{1,0:T(8,128)}, f32[512,256]{1,0:T(8,128)}, f32[88,256]{1,0:T(8,128)}) custom-call(f32[128,256]{1,0:T(8,128)} %r1_hbm.1, f32[128,256]{1,0:T(8,128)} %r2_hbm.1, f32[88,256]{1,0:T(8,128)} %rest_hbm.1, bf16[512,128]{1,0:T(8,128)(2,1)} %inv1_hbm.1, bf16[512,128]{1,0:T(8,128)(2,1)} %inv2_hbm.1, bf16[128,512]{1,0:T(8,128)(2,1)} %cross_hbm.1, ...), custom_call_target="tpu_custom_call" | custom-call | flops 1000000000 | bytes 5000000 | tf_op jit(solution)/shard_map/pallas_call | solution.py:292
  86.6 2.1 %shard_map.104 = (f32[512,256]{1,0:T(8,128)}, f32[512,256]{1,0:T(8,128)}, f32[88,256]{1,0:T(8,128)}) custom-call(f32[512,256]{1,0:T(8,128)} %get-tuple-element.6.a1, f32[512,256]{1,0:T(8,128)} %get-tuple-element.7.a2, f32[88,256]{1,0:T(8,128)} %get-tuple-element.8.a3), custom_call_target="tpu_custom_call" | custom-call | tf_op jit(solution)/shard_map/pallas_call | solution.py:325
